TPU v7x, 512 devices: a whole 4x4x16 slice. The times are simulated.
512 devices in a mesh: dp: 4 (over y), dev: 128 (over x, z, core).
Axes of the slice: x: 4, y: 4, z: 16, core: 2. Of those that a mesh axis runs over, the one named last changes fastest.
Arguments:
- frames: bfloat16 [512, 48, 8192], P(('dp', 'dev')), parts along dimension 0, may hold values from -6 to 6
- clip_ids: int32 [512], P(('dp', 'dev')), parts along dimension 0, may hold values from 0 to 11, never falling along the last dimension, each value on 1 to 17 neighbouring positions
- norm_gain: float32 [2, 64], replicated, may hold values from 0.25 to 1.75
- space_kernel: bfloat16 [2, 3, 3, 64, 64], replicated, may hold values from -0.25 to 0.25
- time_kernel: bfloat16 [2, 5, 64, 64], replicated, may hold values from -0.3125 to 0.3125
Outputs:
- encoded: bfloat16 [512, 48, 8192], P(('dp', 'dev')), parts along dimension 0
There are 4 independent parts, one for each index of `dp`. A program takes and returns all parts, laid end to end along the dimension named above; an argument that names none is the same for every part. Nothing has to cross between parts.
Inputs may be any that keep to these rules, and one draw needn't show every extreme that they name: `clip_ids`: clip ids never fall along the frames; each clip holds 1 to 17 frames, one exactly 17.
All inputs are finite; a program needn't handle non-finite values.
Results may differ from a plain program's by a relative error of at most 0.0061.
Values may be sent and summed in bfloat16 or wider, within the bound.
A program may use at most 64 MiB of HBM per device.

v0:
```python
import jax
import jax.numpy as jnp
from jax import lax
from jax.sharding import PartitionSpec as P

GROUPS = 32
TIME_TAPS = 5
TIME_DILATION = 2
BLOCKS = 2


def slide_frames(source, frame_offset):
    if frame_offset == 0:
        return source
    blank = jnp.zeros((abs(frame_offset),) + source.shape[1:], source.dtype)
    if frame_offset > 0:
        return jnp.concatenate([source[frame_offset:], blank], 0)
    return jnp.concatenate([blank, source[: source.shape[0] + frame_offset]], 0)


def pair_bands(kernel):
    width = kernel.shape[-1]
    blank = jnp.zeros((width, width), kernel.dtype)
    bands = []
    for r in range(3):
        for d in (-1, 0, 1):
            stacked = []
            for a in (0, 1):
                placed = []
                for b in (0, 1):
                    q = 2 * d + a - b + 1
                    placed.append(kernel[r, q] if 0 <= q <= 2 else blank)
                stacked.append(jnp.concatenate(placed, 1))
            bands.append(jnp.concatenate(stacked, 0))
    return bands


def paired_diagonal(matrix):
    blank = jnp.zeros_like(matrix)
    upper = jnp.concatenate([matrix, blank], 1)
    lower = jnp.concatenate([blank, matrix], 1)
    return jnp.concatenate([upper, lower], 0)


def normed(values, gain):
    local = values.shape[0]
    height = values.shape[1]
    width = gain.shape[0]
    columns = values.shape[2] // width
    per_group = width // GROUPS
    table_entries = height * columns * per_group
    floats = values.astype(jnp.float32)
    summed = jnp.sum(floats, axis=1).reshape(local, columns, GROUPS, per_group).sum(axis=(1, 3))
    center = jnp.tile(jnp.repeat(summed / table_entries, per_group, axis=1), (1, columns))
    shifted = floats - center[:, None, :]
    squares = (
        jnp.sum(shifted * shifted, axis=1)
        .reshape(local, columns, GROUPS, per_group)
        .sum(axis=(1, 3))
    )
    scale = jnp.tile(
        jnp.repeat(lax.rsqrt(squares / table_entries + 1e-06), per_group, axis=1), (1, columns)
    )
    gains = jnp.tile(gain, columns)
    return jax.nn.silu(shifted * scale[:, None, :] * gains).astype(jnp.bfloat16)


def spatial_convolve(act, bands, width):
    local = act.shape[0]
    height = act.shape[1]
    halves = act.shape[2] // (2 * width)
    paired = act.reshape(local, height, halves, 2 * width)
    padded = jnp.pad(paired, ((0, 0), (1, 1), (1, 1), (0, 0)))
    total = jnp.zeros((local * height * halves, 2 * width), jnp.float32)
    for r in range(3):
        for d in (-1, 0, 1):
            window = padded[:, r : r + height, d + 1 : d + 1 + halves, :].reshape(-1, 2 * width)
            total = total + jnp.dot(
                window, bands[r * 3 + d + 1], preferred_element_type=jnp.float32
            )
    return total.astype(jnp.bfloat16).reshape(local, height * halves, 2 * width)


def per_device(frames, clip_ids, norm_gain, space_kernel, time_kernel):
    table = lax.all_gather(clip_ids, "dev", axis=0, tiled=True)
    marks = table + 1
    local = frames.shape[0]
    width = space_kernel.shape[-1]
    devices = lax.axis_size("dev")
    frame_offsets = [
        (kernel_step - TIME_TAPS // 2) * TIME_DILATION for kernel_step in range(TIME_TAPS)
    ]
    current = frames
    for block_index in range(BLOCKS):
        bands = pair_bands(space_kernel[block_index])
        pairs = [
            paired_diagonal(time_kernel[block_index, kernel_step])
            for kernel_step in range(TIME_TAPS)
        ]
        act = normed(current, norm_gain[block_index])
        spat = spatial_convolve(act, bands, width)
        masks = [
            (slide_frames(marks, frame_offset) == marks).astype(jnp.bfloat16)
            for frame_offset in frame_offsets
        ]
        tiled = spat.reshape(local, devices, spat.shape[1] // devices, 2 * width)
        stack = lax.all_to_all(tiled, "dev", split_axis=1, concat_axis=0, tiled=True)
        total = jnp.zeros(
            (stack.shape[0] * stack.shape[1] * stack.shape[2], 2 * width), jnp.float32
        )
        for along_kernel_step in range(TIME_TAPS):
            moved = (
                slide_frames(stack, frame_offsets[along_kernel_step])
                * masks[along_kernel_step][:, None, None, None]
            )
            total = total + jnp.dot(
                moved.reshape(-1, 2 * width),
                pairs[along_kernel_step],
                preferred_element_type=jnp.float32,
            )
        tiles = total.astype(jnp.bfloat16).reshape(stack.shape)
        update = lax.all_to_all(tiles, "dev", split_axis=0, concat_axis=1, tiled=True)
        summed = current.astype(jnp.float32) + update.reshape(current.shape).astype(jnp.float32)
        current = summed.astype(jnp.bfloat16)
    return current


def solution(mesh):
    return jax.shard_map(
        per_device,
        mesh=mesh,
        in_specs=(P(("dp", "dev"), None, None), P(("dp", "dev")), P(), P(), P()),
        out_specs=P(("dp", "dev"), None, None),
        check_vma=False,
    )
```

profile of v0, /device:TPU:6, one launch (start us, length us, event | category | flops | bytes accessed | tf_op | source)
XLA Modules:
  0.0 295.5 jit_solution(706999053783665826)
XLA Ops:
  0.0 1.2 slice_bitcast_fusion.38
  1.3 1.3 convert_reduce_fusion.1
  2.6 3.4 %reshape.258 = f32[128,32,2]{2,1,0:T(8,128)} reshape(f32[8192]{0:T(1024)S(1)} %convert_reduce_fusion.1) | data formatting | bytes 65536 | tf_op jit(solution)/shard_map/reshape | solution.py:53
  6.0 2.0 reduce_sum.73
  8.6 3.4 %reshape.259 = f32[128,32,2]{2,1,0:T(8,128)} reshape(f32[8192]{0:T(1024)S(1)} %fusion.16) | data formatting | bytes 65536 | tf_op jit(solution)/shard_map/reshape | solution.py:58
  12.0 1.9 reduce_sum.75
  15.4 3.3 %pad_slice_fusion.8 = (bf16[1,48,64,128]{3,2,1,0:T(8,128)(2,1)S(1)}, bf16[1,48,64,128]{3,2,1,0:T(8,128)(2,1)}, bf16[1,48,64,128]{3,2,1,0:T(8,128)(2,1)}, bf16[1,...) fusion(bf16[1,48,64,128]{3,2,1,0:T(8,128)(2,1)S(1)} %bitcast.172), kind=kLoop, calls=%fused_computation.80 | loop fusion | bytes 7077888 | tf_op jit(solution)/shard_map/slice | solution.py:77
  18.8 1.3 reshape.265
  23.8 0.8 copy-done.13
  27.2 0.8 copy-done.1
  28.4 1.3 fusion
  29.7 20.0 %all-to-all-start = ((bf16[1,128,24,128]{3,2,0,1:T(8,128)(2,1)}), bf16[1,128,24,128]{3,2,0,1:T(8,128)(2,1)S(1)}, u32[]{:S(2)}, u32[]{:S(2)}) async-start(bf16[1,128,24,128]{3,2,0,1:T(8,128)(2,1)} %bitcast.20), calls=%async_computation | async-start | bytes 1572864 | tf_op jit(solution)/shard_map/all_to_all | solution.py:107
  50.4 1.3 dynamic-slice
  52.5 52.3 %all-reduce.58 = s32[128]{0:T(128)S(1)} all-reduce(s32[128]{0:T(128)S(1)} %dynamic-update-slice), channel_id=1, replica_groups=mesh['dp'=4,'dev'=128] {'dev'}, use_global_device_ids=true, to_apply=%add.58 | all-reduce | flops 128 | bytes 1024
  107.9 1.3 fusion.1
  109.2 15.1 %all-to-all-start.1 = ((bf16[128,1,24,128]{3,2,1,0:T(8,128)(2,1)}), bf16[128,1,24,128]{3,2,1,0:T(8,128)(2,1)S(1)}, u32[]{:S(2)}, u32[]{:S(2)}) async-start(bf16[128,1,24,128]{3,2,1,0:T(8,128)(2,1)} %bitcast.38), calls=%async_computation.1 | async-start | bytes 1572864 | tf_op jit(solution)/shard_map/all_to_all | solution.py:122
  124.5 42.9 %all-to-all-done.1 = bf16[128,1,24,128]{3,2,1,0:T(8,128)(2,1)S(1)} async-done(((bf16[128,1,24,128]{3,2,1,0:T(8,128)(2,1)}), bf16[128,1,24,128]{3,2,1,0:T(8,128)(2,1)S(1)}, u32[]{:S(2)}, u32[]{:S(2)}) %all-to-all-start.1) | async-done | bytes 786464 | tf_op jit(solution)/shard_map/all_to_all | solution.py:122
  167.9 2.1 reshape.276
  170.9 2.1 reshape.277
  174.8 3.3 %pad_slice_fusion = (bf16[1,48,64,128]{3,2,1,0:T(8,128)(2,1)S(1)}, bf16[1,48,64,128]{3,2,1,0:T(8,128)(2,1)}, bf16[1,48,64,128]{3,2,1,0:T(8,128)(2,1)}, bf16[1,48...) fusion(bf16[1,48,64,128]{3,2,1,0:T(8,128)(2,1)S(1)} %bitcast.173), kind=kLoop, calls=%fused_computation.72 | loop fusion | bytes 7077888 | tf_op jit(solution)/shard_map/slice | solution.py:77
  178.1 1.2 reshape.283
  188.2 51.4 %all_to_all.42 = bf16[1,128,24,128]{3,2,0,1:T(8,128)(2,1)S(1)} all-to-all(bf16[1,128,24,128]{3,2,0,1:T(8,128)(2,1)S(1)} %bitcast.181), channel_id=1, replica_groups=mesh['dp'=4,'dev'=128] {'dev'}, dimensions={1} | all-to-all | bytes 1572864 | tf_op jit(solution)/shard_map/all_to_all | solution.py:107
  242.8 51.4 %all_to_all.43 = bf16[128,1,24,128]{3,2,1,0:T(8,128)(2,1)S(1)} all-to-all(bf16[128,1,24,128]{3,2,1,0:T(8,128)(2,1)S(1)} %bitcast.182), channel_id=1, replica_groups=mesh['dp'=4,'dev'=128] {'dev'}, dimensions={0} | all-to-all | bytes 1572864 | tf_op jit(solution)/shard_map/all_to_all | solution.py:122
  294.5 1.0 fusion.25
  (125 shorter events, 28.2 us)
Async XLA Ops:
  6.0 2.3 copy-start
  15.4 3.3 %copy-start.15 = (bf16[2,3,3,64,64]{4,3,2,1,0:T(8,128)(2,1)S(1)}, bf16[2,3,3,64,64]{4,3,2,1,0:T(8,128)(2,1)}, u32[]{:S(2)}) copy-start(bf16[2,3,3,64,64]{4,3,2,1,0:T(8,128)(2,1)} %param.8) | copy-start | bytes 442372
  20.0 1.1 copy-start.6
  21.2 1.1 copy-start.5
  22.3 1.1 copy-start.4
  23.4 1.1 copy-start.13
  24.6 1.1 copy-start.3
  25.7 1.1 copy-start.2
  26.9 1.1 copy-start.1
  29.7 75.3 %copy-start.16 = (bf16[2,5,64,64]{3,2,1,0:T(8,128)(2,1)S(1)}, bf16[2,5,64,64]{3,2,1,0:T(8,128)(2,1)}, u32[]{:S(2)}) copy-start(bf16[2,5,64,64]{3,2,1,0:T(8,128)(2,1)} %param.9) | copy-start | bytes 245764
  29.7 75.3 %all-to-all-start = ((bf16[1,128,24,128]{3,2,0,1:T(8,128)(2,1)}), bf16[1,128,24,128]{3,2,0,1:T(8,128)(2,1)S(1)}, u32[]{:S(2)}, u32[]{:S(2)}) async-start(bf16[1,128,24,128]{3,2,0,1:T(8,128)(2,1)} %bitcast.20), calls=%async_computation | async-start | bytes 1572864 | tf_op jit(solution)/shard_map/all_to_all | solution.py:107
  109.2 15.1 %copy-start.19 = (f32[64]{0:T(128)S(1)}, f32[64]{0:T(128)}, u32[]{:S(2)}) copy-start(f32[64]{0:T(128)} %get-tuple-element.57) | copy-start | bytes 772
  109.2 58.1 %all-to-all-start.1 = ((bf16[128,1,24,128]{3,2,1,0:T(8,128)(2,1)}), bf16[128,1,24,128]{3,2,1,0:T(8,128)(2,1)S(1)}, u32[]{:S(2)}, u32[]{:S(2)}) async-start(bf16[128,1,24,128]{3,2,1,0:T(8,128)(2,1)} %bitcast.38), calls=%async_computation.1 | async-start | bytes 1572864 | tf_op jit(solution)/shard_map/all_to_all | solution.py:122
  179.4 1.1 copy-start.12
  179.4 1.1 copy-start.18
  180.5 1.1 copy-start.11
  181.6 1.1 copy-start.10
  182.8 1.1 copy-start.14
  182.8 1.1 copy-start.17
  183.9 1.1 copy-start.9
  185.0 1.1 copy-start.8
  186.2 1.1 copy-start.7
where the time goes:
time: 298 us; the launch traced here: 296 us
  blocking collectives  155 us (52%)
  waiting for transfers between devices  42.9 us (14%)
  local copies, waits for them, and re-layouts  37 us (12%)
  starting transfers between devices  35.1 us (12%)
  matrix products  13 us (4%)
  other arithmetic  11.3 us (4%)
    unnamed x1, blocking collectives  52.3 us
    all_to_all x1, blocking collectives, per_device(): lax.all_to_all(tiled, 'dev', split_axis=1, concat_axis=0, tiled=True)  51.4 us
    all_to_all x1, blocking collectives, per_device(): lax.all_to_all(tiles, 'dev', split_axis=0, concat_axis=1, tiled=True)  51.4 us
    all_to_all x1, waiting for transfers between devices, per_device(): lax.all_to_all(tiles, 'dev', split_axis=0, concat_axis=1, tiled=True)  42.9 us
    all_to_all x1, starting transfers between devices, per_device(): lax.all_to_all(tiled, 'dev', split_axis=1, concat_axis=0, tiled=True)  20 us
    all_to_all x1, starting transfers between devices, per_device(): lax.all_to_all(tiles, 'dev', split_axis=0, concat_axis=1, tiled=True)  15.1 us
    unnamed x45, local copies, waits for them, and re-layouts  12.2 us
    dot_general x18, matrix products, spatial_convolve(): jnp.dot(window, bands[r * 3 + d + 1], preferred_element_type=jnp.float32)  7.94 us
  transfers between devices with their start and end apart: 2, of which 1 were waited for; matrix products, arithmetic and copies ran while one was open for 1% of the time, Pallas kernels for 0%

commit v1 on v0

v1 whole, which is shorter than its diff:
```python
import jax
import jax.numpy as jnp
from jax import lax
from jax.experimental import pallas as pl
from jax.experimental.pallas import tpu as pltpu
from jax.sharding import PartitionSpec as P

BLOCKS = 2
TAPS = 5
STEP = 2
GROUP = 2
PIECES = 8
EPS = 1e-06
MESH = pl.DeviceIdType.MESH
F32 = jnp.float32
BF16 = jnp.bfloat16
OFFSETS = (STEP, -STEP, 2 * STEP, -2 * STEP)
SLOT_OF_TAP = (2, 0, None, 1, 3)


def kernel(
    frames, clip, gain, space, time, out,
    x_buf, shifted, act, spat, came, bands, taps, my_id, ids, out_buf,
    send_sem, recv_sem, id_send, id_recv, out_sem,
):
    count = lax.axis_size("dev")
    me = lax.axis_index("dev")
    tiles, rows, lanes = x_buf.shape
    half = lanes // 2
    span = tiles // PIECES
    table_entries = rows * tiles * 2 * GROUP

    def peer(offset):
        return {"dev": lax.rem(me + offset + count, count)}

    barrier = pltpu.get_barrier_semaphore()
    for offset in OFFSETS:
        pl.semaphore_signal(barrier, inc=1, device_id=peer(offset), device_id_type=MESH)

    lane = lax.broadcasted_iota(jnp.int32, (1, lanes), 1)

    def whole_group(sums):
        both = sums + pltpu.roll(sums, half, 1)
        beside = jnp.where(lane % 2 == 0, pltpu.roll(both, lanes - 1, 1), pltpu.roll(both, 1, 1))
        return both + beside

    def piece(p):
        return pl.ds(pl.multiple_of(p * span, span), span)

    def take(p, sums):
        for t in range(span):
            at = pl.multiple_of((p * span + t) * lanes, lanes)
            tile = frames[0, :, pl.ds(at, lanes)]
            x_buf[p * span + t] = tile
            sums = sums + jnp.sum(tile.astype(F32), axis=0, keepdims=True)
        return sums

    sums = lax.fori_loop(0, PIECES, take, jnp.zeros((1, lanes), F32))

    my_id[...] = jnp.full(my_id.shape, clip[0], jnp.int32)
    shifted[...] = jnp.zeros_like(shifted)
    for r in range(3):
        act[r, 0] = jnp.zeros((rows, lanes), BF16)
        act[r, tiles + 1] = jnp.zeros((rows, lanes), BF16)
    bands[...] = jnp.zeros_like(bands)
    taps[...] = jnp.zeros_like(taps)

    def fill_bands(b):
        for r in range(3):
            for d in range(3):
                for a in range(2):
                    for c in range(2):
                        q = 2 * (d - 1) + a - c + 1
                        if 0 <= q <= 2:
                            at = (r * 3 + d) * lanes + a * half
                            bands[b, at : at + half, c * half : (c + 1) * half] = space[b, r, q]

    fill_bands(0)

    def id_copy(slot):
        return pltpu.make_async_remote_copy(
            src_ref=my_id, dst_ref=ids.at[slot], send_sem=id_send.at[slot], recv_sem=id_recv.at[slot],
            device_id=peer(OFFSETS[slot]), device_id_type=MESH,
        )

    def copy(b, slot, p):
        source = spat.at[b] if slot < 2 else came.at[b, slot - 2]
        return pltpu.make_async_remote_copy(
            src_ref=source.at[piece(p)], dst_ref=came.at[b, slot, piece(p)],
            send_sem=send_sem.at[b, slot, p], recv_sem=recv_sem.at[b, slot, p],
            device_id=peer(OFFSETS[slot % 2]), device_id_type=MESH,
        )

    def write_out(p):
        wide = span * lanes
        return pltpu.make_async_copy(
            out_buf.at[p], out.at[0, :, pl.ds(pl.multiple_of(p * wide, wide), wide)], out_sem.at[p]
        )

    for b in range(BLOCKS):
        mean = whole_group(sums) / table_entries

        def squares(p, total):
            off = x_buf[piece(p)].astype(F32) - mean
            return total + jnp.sum(off * off, axis=(0, 1))[None]

        spread = whole_group(lax.fori_loop(0, PIECES, squares, jnp.zeros((1, lanes), F32))) / table_entries
        gains = gain[b][None]
        scale = lax.rsqrt(spread + EPS) * jnp.concatenate([gains, gains], 1) * 0.5

        def activate(p):
            u = (x_buf[piece(p)].astype(F32) - mean) * scale
            value = u * (1.0 + jnp.tanh(u))
            shifted[:, 8 : 8 + rows] = value
            at = pl.ds(p * span + 1, span)
            act[1, at] = value.astype(BF16)
            act[0, at] = shifted[:, 7 : 7 + rows].astype(BF16)
            act[2, at] = shifted[:, 9 : 9 + rows].astype(BF16)

        def convolve(p):
            window = jnp.concatenate(
                [act[r, pl.ds(p * span + d, span)].reshape(span * rows, lanes) for r in range(3) for d in range(3)], 1
            )
            total = jnp.dot(window, bands[b], preferred_element_type=F32)
            spat[b, piece(p)] = total.astype(BF16).reshape(span, rows, lanes)

        activate(0)

        def make(p, carry):
            @pl.when(p + 1 < PIECES)
            def _():
                activate(p + 1)

            convolve(p)
            if b == 0:

                @pl.when(p == 0)
                def _():
                    pl.semaphore_wait(barrier, len(OFFSETS))

            copy(b, 0, p).start()
            copy(b, 1, p).start()
            return carry

        lax.fori_loop(0, PIECES, make, 0)

        if b == 0:
            for slot in range(4):
                id_copy(slot).start()
            for later in range(1, BLOCKS):
                fill_bands(later)
            for slot in range(4):
                id_copy(slot).wait()
            for k in range(TAPS):
                slot = SLOT_OF_TAP[k]
                for c in range(BLOCKS):
                    if slot is None:
                        matrix = time[c, k]
                    else:
                        other = me + (k - TAPS // 2) * STEP
                        inside = jnp.logical_and(other >= 0, other < count).astype(jnp.int32)
                        same = (ids[slot] == my_id[...]).astype(jnp.int32) * inside
                        keep = same[:1, :half].astype(F32)
                        matrix = (time[c, k].astype(F32) * keep).astype(BF16)
                    for a in range(2):
                        at = k * lanes + a * half
                        taps[c, at : at + half, a * half : (a + 1) * half] = matrix

        def forward(p, carry):
            for slot in range(2):
                copy(b, slot, p).wait_recv()
                copy(b, slot + 2, p).start()
            return carry

        lax.fori_loop(0, PIECES, forward, 0)

        def finish(p, sums):
            copy(b, 2, p).wait_recv()
            copy(b, 3, p).wait_recv()
            window = jnp.concatenate(
                [
                    (spat[b, piece(p)] if slot is None else came[b, slot, piece(p)]).reshape(span * rows, lanes)
                    for slot in SLOT_OF_TAP
                ],
                1,
            )
            update = jnp.dot(window, taps[b], preferred_element_type=F32).astype(BF16).astype(F32)
            value = (x_buf[piece(p)].astype(F32) + update.reshape(span, rows, lanes)).astype(BF16)
            if b + 1 < BLOCKS:
                x_buf[piece(p)] = value
                return sums + jnp.sum(value.astype(F32), axis=(0, 1))[None]
            for t in range(span):
                out_buf[p, :, t * lanes : (t + 1) * lanes] = value[t]
            write_out(p).start()
            return sums

        sums = lax.fori_loop(0, PIECES, finish, jnp.zeros((1, lanes), F32))

    def drain(p, carry):
        for b in range(BLOCKS):
            for slot in range(4):
                copy(b, slot, p).wait_send()
        write_out(p).wait()
        return carry

    lax.fori_loop(0, PIECES, drain, 0)


def per_device(frames, clip_ids, norm_gain, space_kernel, time_kernel):
    _, rows, wide = frames.shape
    lanes = 2 * space_kernel.shape[-1]
    tiles = wide // lanes
    span = tiles // PIECES
    vmem = pl.BlockSpec(memory_space=pltpu.VMEM)
    return pl.pallas_call(
        kernel,
        out_shape=jax.ShapeDtypeStruct(frames.shape, BF16),
        in_specs=[vmem, pl.BlockSpec(memory_space=pltpu.SMEM), vmem, vmem, vmem],
        out_specs=pl.BlockSpec(memory_space=pl.ANY),
        scratch_shapes=[
            pltpu.VMEM((tiles, rows, lanes), BF16),
            pltpu.VMEM((span, rows + 16, lanes), F32),
            pltpu.VMEM((3, tiles + 2, rows, lanes), BF16),
            pltpu.VMEM((BLOCKS, tiles, rows, lanes), BF16),
            pltpu.VMEM((BLOCKS, 4, tiles, rows, lanes), BF16),
            pltpu.VMEM((BLOCKS, 9 * lanes, lanes), BF16),
            pltpu.VMEM((BLOCKS, TAPS * lanes, lanes), BF16),
            pltpu.VMEM((8, lanes), jnp.int32),
            pltpu.VMEM((4, 8, lanes), jnp.int32),
            pltpu.VMEM((PIECES, rows, span * lanes), BF16),
            pltpu.SemaphoreType.DMA((BLOCKS, 4, PIECES)),
            pltpu.SemaphoreType.DMA((BLOCKS, 4, PIECES)),
            pltpu.SemaphoreType.DMA((4,)),
            pltpu.SemaphoreType.DMA((4,)),
            pltpu.SemaphoreType.DMA((PIECES,)),
        ],
        compiler_params=pltpu.CompilerParams(
            collective_id=0, has_side_effects=True, vmem_limit_bytes=40 << 20
        ),
        cost_estimate=pl.CostEstimate(flops=4_000_000_000, bytes_accessed=2_000_000, transcendentals=800_000),
    )(frames, clip_ids, norm_gain, space_kernel, time_kernel)


def solution(mesh):
    return jax.shard_map(
        per_device,
        mesh=mesh,
        in_specs=(P(("dp", "dev"), None, None), P(("dp", "dev")), P(), P(), P()),
        out_specs=P(("dp", "dev"), None, None),
        check_vma=False,
    )
```

time: 298 us -> 95.6 us (0.32)
  the two profiles are of different devices: /device:TPU:6 before, /device:TPU:24 now
where the time goes in v1:
time: 95.6 us; the launch traced here: 95.4 us
  Pallas kernels  90.8 us (95%)
  local copies, waits for them, and re-layouts  3.9 us (4%)
    pallas_call x1, Pallas kernels, per_device(): pl.pallas_call(kernel, out_shape=jax.ShapeDtypeStruct(frames.shape, BF16)...  90.8 us
    unnamed x9, local copies, waits for them, and re-layouts  3.9 us

profile of v1, /device:TPU:24, one launch (start us, length us, event | category | flops | bytes accessed | tf_op | source)
XLA Modules:
  0.0 95.4 jit_solution(652335753152274735)
XLA Ops:
  0.0 0.0 copy-start.3
  0.7 0.0 copy-done.3
  0.7 0.0 copy-start
  0.7 1.1 %copy-done = bf16[1,48,8192]{2,1,0:T(8,128)(2,1)S(1)} copy-done((bf16[1,48,8192]{2,1,0:T(8,128)(2,1)S(1)}, bf16[1,48,8192]{2,1,0:T(8,128)(2,1)}, u32[]{:S(2)}) %copy-start) | copy-done | bytes 786456
  1.8 0.0 copy-start.1
  1.8 1.0 %copy-done.1 = bf16[2,3,3,64,64]{4,3,2,1,0:T(8,128)(2,1)S(1)} copy-done((bf16[2,3,3,64,64]{4,3,2,1,0:T(8,128)(2,1)S(1)}, bf16[2,3,3,64,64]{4,3,2,1,0:T(8,128)(2,1)}, u32[]{:S(2)}) %copy-start.1) | copy-done | bytes 147480
  2.8 0.0 copy-start.2
  2.8 0.9 copy-done.2
  3.7 90.8 %shard_map.55 = bf16[1,48,8192]{2,1,0:T(8,128)(2,1)S(1)} custom-call(bf16[1,48,8192]{2,1,0:T(8,128)(2,1)S(1)} %copy-done, s32[1]{0:T(128)S(6)} %copy.7.clip, f32[2,64]{1,0:T(2,128)S(1)} %copy-done.3, bf16[2,3,3,64,64]{4,3,2,1,0:T(8,128)(2,1)S(1)} %copy-done.1, bf16[2,5,64,64]{3,2,1,0:T(8,128)(2,1)S(1)} %copy-done.2), custom_call_target="tpu_custom_call" | custom-call | flops 4000000000 | bytes 2000000 | tf_op jit(solution)/shard_map/pallas_call | solution.py:215
  94.5 0.9 copy.8
Async XLA Ops:
  0.0 0.7 copy-start.3
  0.7 1.1 %copy-start = (bf16[1,48,8192]{2,1,0:T(8,128)(2,1)S(1)}, bf16[1,48,8192]{2,1,0:T(8,128)(2,1)}, u32[]{:S(2)}) copy-start(bf16[1,48,8192]{2,1,0:T(8,128)(2,1)} %frames.1) | copy-start | bytes 2359300
  1.8 1.0 %copy-start.1 = (bf16[2,3,3,64,64]{4,3,2,1,0:T(8,128)(2,1)S(1)}, bf16[2,3,3,64,64]{4,3,2,1,0:T(8,128)(2,1)}, u32[]{:S(2)}) copy-start(bf16[2,3,3,64,64]{4,3,2,1,0:T(8,128)(2,1)} %space.1) | copy-start | bytes 442372
  2.8 0.9 copy-start.2

commit v2 on v1

v2 whole, which is shorter than its diff:
```python
import jax
import jax.numpy as jnp
from jax import lax
from jax.experimental import pallas as pl
from jax.experimental.pallas import tpu as pltpu
from jax.sharding import PartitionSpec as P

BLOCKS = 2
TAPS = 5
STEP = 2
GROUP = 2
PIECES = 16
EARLY = 3
RAW_AT = 6
EPS = 1e-06
MESH = pl.DeviceIdType.MESH
F32 = jnp.float32
BF16 = jnp.bfloat16
OFFSETS = (STEP, -STEP, 2 * STEP, -2 * STEP)
SLOT_OF_TAP = (2, 0, None, 1, 3)


def kernel(
    frames_hbm, clip, gain_hbm, space_hbm, time_hbm, out,
    frames, gain, space, time,
    x_buf, shifted, act, spat, came, raw, bands, taps, facts, facts_in,
    load_sem, frame_sem, send_sem, recv_sem, raw_send, raw_recv, fact_send, fact_recv,
):
    count = lax.axis_size("dev")
    me = lax.axis_index("dev")
    tiles, rows, lanes = x_buf.shape
    half = lanes // 2
    span = tiles // PIECES
    wide = span * lanes
    early = raw.shape[2]
    table_entries = rows * tiles * 2 * GROUP

    def peer(offset):
        return {"dev": lax.rem(me + offset + count, count)}

    def here(offset):
        return jnp.logical_and(me + offset >= 0, me + offset < count)

    takes = [here(-offset) for offset in OFFSETS]
    gives = [here(STEP), here(-STEP)]
    gives += [jnp.logical_and(gives[0], takes[0]), jnp.logical_and(gives[1], takes[1])]

    def if_so(condition, action):
        pl.when(condition)(action)

    barrier = pltpu.get_barrier_semaphore()
    for offset in OFFSETS:

        @pl.when(here(offset))
        def _():
            pl.semaphore_signal(barrier, inc=1, device_id=peer(offset), device_id_type=MESH)

    def piece(p):
        return pl.ds(pl.multiple_of(p * span, span), span)

    def fetch(p):
        at = pl.ds(pl.multiple_of(p * wide, wide), wide)
        return pltpu.make_async_copy(frames_hbm.at[0, :, at], frames.at[:, at], frame_sem.at[p])

    def start_fetch(p, carry):
        fetch(p).start()
        return carry

    lax.fori_loop(0, PIECES, start_fetch, 0)
    loads = [
        pltpu.make_async_copy(source, target, load_sem.at[i])
        for i, (source, target) in enumerate(
            ((space_hbm, space), (gain_hbm, gain), (time_hbm, time))
        )
    ]
    for load in loads:
        load.start()

    def copy(b, slot, p):
        source = spat.at[b] if slot < 2 else came.at[b, slot - 2]
        return pltpu.make_async_remote_copy(
            src_ref=source.at[piece(p)], dst_ref=came.at[b, slot, piece(p)],
            send_sem=send_sem.at[b, slot, p], recv_sem=recv_sem.at[b, slot, p],
            device_id=peer(OFFSETS[slot % 2]), device_id_type=MESH,
        )

    def raw_copy(b, slot):
        source = x_buf.at[pl.ds(0, early)] if slot < 2 else raw.at[b, slot - 2]
        return pltpu.make_async_remote_copy(
            src_ref=source, dst_ref=raw.at[b, slot],
            send_sem=raw_send.at[b, slot], recv_sem=raw_recv.at[b, slot],
            device_id=peer(OFFSETS[slot % 2]), device_id_type=MESH,
        )

    def fact_copy(b, slot):
        return pltpu.make_async_remote_copy(
            src_ref=facts.at[b], dst_ref=facts_in.at[b, slot],
            send_sem=fact_send.at[b, slot], recv_sem=fact_recv.at[b, slot],
            device_id=peer(OFFSETS[slot]), device_id_type=MESH,
        )

    lane = lax.broadcasted_iota(jnp.int32, (1, lanes), 1)

    def whole_group(sums):
        both = sums + pltpu.roll(sums, half, 1)
        beside = jnp.where(lane % 2 == 0, pltpu.roll(both, lanes - 1, 1), pltpu.roll(both, 1, 1))
        return both + beside

    def take(p, sums):
        fetch(p).wait()
        for t in range(span):
            at = pl.multiple_of((p * span + t) * lanes, lanes)
            tile = frames[:, pl.ds(at, lanes)]
            x_buf[p * span + t] = tile
            sums = sums + jnp.sum(tile.astype(F32), axis=0, keepdims=True)
        return sums

    sums = lax.fori_loop(0, EARLY + 1, take, jnp.zeros((1, lanes), F32))
    pl.semaphore_wait(barrier, sum(here(offset).astype(jnp.int32) for offset in OFFSETS))
    for slot in range(2):
        if_so(gives[slot], raw_copy(0, slot).start)
    sums = lax.fori_loop(EARLY + 1, PIECES, take, sums)

    shifted[...] = jnp.zeros_like(shifted)
    for r in range(3):
        act[r, 0] = jnp.zeros((rows, lanes), BF16)
        act[r, tiles + 1] = jnp.zeros((rows, lanes), BF16)
    bands[...] = jnp.zeros_like(bands)

    def fill_bands(b):
        for r in range(3):
            for d in range(3):
                for a in range(2):
                    for c in range(2):
                        q = 2 * (d - 1) + a - c + 1
                        if 0 <= q <= 2:
                            at = (r * 3 + d) * lanes + a * half
                            bands[b, at : at + half, c * half : (c + 1) * half] = space[b, r, q]

    def activate(values, at, mean, scale):
        n = values.shape[0]
        u = (values.astype(F32) - mean) * scale
        value = u * (1.0 + jnp.tanh(u))
        shifted[:n, 8 : 8 + rows] = value
        where = pl.ds(at + 1, n)
        act[1, where] = value.astype(BF16)
        act[0, where] = shifted[:n, 7 : 7 + rows].astype(BF16)
        act[2, where] = shifted[:n, 9 : 9 + rows].astype(BF16)

    def convolve(b, p):
        window = jnp.concatenate(
            [act[r, pl.ds(p * span + d, span)].reshape(span * rows, lanes) for r in range(3) for d in range(3)], 1
        )
        total = jnp.dot(window, bands[b], preferred_element_type=F32)
        return total.astype(BF16).reshape(span, rows, lanes)

    loads[0].wait()
    fill_bands(0)
    loads[1].wait()

    for b in range(BLOCKS):
        mean = whole_group(sums) / table_entries

        def squares(p, total):
            off = x_buf[piece(p)].astype(F32) - mean
            return total + jnp.sum(off * off, axis=(0, 1))[None]

        spread = whole_group(lax.fori_loop(0, PIECES, squares, jnp.zeros((1, lanes), F32))) / table_entries
        gains = gain[b : b + 1]
        scale = lax.rsqrt(spread + EPS) * jnp.concatenate([gains, gains], 1) * 0.5
        facts[b, 0:1] = mean
        facts[b, 1:2] = scale
        facts[b, 2:8] = jnp.full((6, lanes), clip[0], jnp.int32).astype(F32)
        for slot in range(4):
            if_so(here(OFFSETS[slot]), fact_copy(b, slot).start)

        def own(p):
            activate(x_buf[piece(p)], p * span, mean, scale)

        own(EARLY - 1)
        own(EARLY)

        def make(p, carry):
            @pl.when(p + 1 < PIECES)
            def _():
                own(p + 1)

            spat[b, piece(p)] = convolve(b, p)
            for slot in range(2):
                if_so(gives[slot], copy(b, slot, p).start)
            return carry

        lax.fori_loop(EARLY, PIECES, make, 0)

        for slot in range(2):
            if_so(takes[slot], raw_copy(b, slot).wait_recv)
            if_so(gives[slot + 2], raw_copy(b, slot + 2).start)

        def own_early(p, carry):
            own(p)
            return carry

        lax.fori_loop(0, EARLY - 1, own_early, 0)

        def make_early(p, carry):
            spat[b, piece(p)] = convolve(b, p)
            return carry

        lax.fori_loop(0, EARLY, make_early, 0)

        def redo(slot):
            if slot > 1:
                raw_copy(b, slot).wait_recv()
            fact_copy(b, slot).wait_recv()
            mean = facts_in[b, slot, 0:1]
            scale = facts_in[b, slot, 1:2]

            def norm(p, carry):
                activate(raw[b, slot, piece(p)], p * span, mean, scale)
                return carry

            lax.fori_loop(0, EARLY, norm, 0)
            activate(raw[b, slot, EARLY * span :], EARLY * span, mean, scale)

            def conv(p, carry):
                came[b, slot, piece(p)] = convolve(b, p)
                return carry

            lax.fori_loop(0, EARLY, conv, 0)

        def redo_or_blank(slot):
            if_so(takes[slot], lambda: redo(slot))

            @pl.when(jnp.logical_not(takes[slot]))
            def _():
                came[b, slot] = jnp.zeros((tiles, rows, lanes), BF16)

        redo_or_blank(0)
        redo_or_blank(1)

        def forward(p, carry):
            for slot in range(2):
                if_so(takes[slot], copy(b, slot, p).wait_recv)
                if_so(gives[slot + 2], copy(b, slot + 2, p).start)
            return carry

        lax.fori_loop(EARLY, PIECES, forward, 0)

        redo_or_blank(2)
        redo_or_blank(3)

        if b == 0:
            for slot in range(2):
                if_so(gives[slot], raw_copy(b, slot).wait_send)
            for later in range(1, BLOCKS):
                fill_bands(later)
            loads[2].wait()
            taps[...] = jnp.zeros_like(taps)
            for k in range(TAPS):
                slot = SLOT_OF_TAP[k]
                for c in range(BLOCKS):
                    if slot is None:
                        matrix = time[c, k]
                    else:
                        inside = here((k - TAPS // 2) * STEP).astype(F32)
                        same = (facts_in[0, slot, 2:3, :half] == facts[0, 2:3, :half]).astype(F32)
                        matrix = (time[c, k].astype(F32) * (same * inside)).astype(BF16)
                    for a in range(2):
                        at = k * lanes + a * half
                        taps[c, at : at + half, a * half : (a + 1) * half] = matrix

        def finish(p, sums):
            window = jnp.concatenate(
                [
                    (spat[b, piece(p)] if slot is None else came[b, slot, piece(p)]).reshape(span * rows, lanes)
                    for slot in SLOT_OF_TAP
                ],
                1,
            )
            update = jnp.dot(window, taps[b], preferred_element_type=F32).astype(BF16).astype(F32)
            value = (x_buf[piece(p)].astype(F32) + update.reshape(span, rows, lanes)).astype(BF16)
            if b + 1 < BLOCKS:
                x_buf[piece(p)] = value
                return sums + jnp.sum(value.astype(F32), axis=(0, 1))[None]
            for t in range(span):
                at = pl.multiple_of((p * span + t) * lanes, lanes)
                out[0, :, pl.ds(at, lanes)] = value[t]
            return sums

        def finish_arrived(p, sums):
            if b + 1 < BLOCKS:

                for slot in range(2):
                    if_so(jnp.logical_and(p == RAW_AT, gives[slot]), raw_copy(b + 1, slot).start)

            for slot in (2, 3):
                if_so(takes[slot], copy(b, slot, p).wait_recv)
            return finish(p, sums)

        sums = lax.fori_loop(0, EARLY, finish, jnp.zeros((1, lanes), F32))
        sums = lax.fori_loop(EARLY, PIECES, finish_arrived, sums)

    for b in range(BLOCKS):
        for slot in range(4):
            if_so(here(OFFSETS[slot]), fact_copy(b, slot).wait_send)
            if b > 0 or slot > 1:
                if_so(gives[slot], raw_copy(b, slot).wait_send)

    def drain(p, carry):
        for b in range(BLOCKS):
            for slot in range(4):
                if_so(gives[slot], copy(b, slot, p).wait_send)
        return carry

    lax.fori_loop(EARLY, PIECES, drain, 0)


def per_device(frames, clip_ids, norm_gain, space_kernel, time_kernel):
    _, rows, wide = frames.shape
    lanes = 2 * space_kernel.shape[-1]
    tiles = wide // lanes
    span = tiles // PIECES
    early = EARLY * span + 1
    hbm = pl.BlockSpec(memory_space=pl.ANY)
    frames, norm_gain, space_kernel, time_kernel = (
        pltpu.with_memory_space_constraint(x, pltpu.HBM) for x in (frames, norm_gain, space_kernel, time_kernel)
    )
    return pl.pallas_call(
        kernel,
        out_shape=jax.ShapeDtypeStruct(frames.shape, BF16),
        in_specs=[hbm, pl.BlockSpec(memory_space=pltpu.SMEM), hbm, hbm, hbm],
        out_specs=pl.BlockSpec(memory_space=pltpu.VMEM),
        scratch_shapes=[
            pltpu.VMEM((rows, wide), BF16),
            pltpu.VMEM(norm_gain.shape, F32),
            pltpu.VMEM(space_kernel.shape, BF16),
            pltpu.VMEM(time_kernel.shape, BF16),
            pltpu.VMEM((tiles, rows, lanes), BF16),
            pltpu.VMEM((span, rows + 16, lanes), F32),
            pltpu.VMEM((3, tiles + 2, rows, lanes), BF16),
            pltpu.VMEM((BLOCKS, tiles, rows, lanes), BF16),
            pltpu.VMEM((BLOCKS, 4, tiles, rows, lanes), BF16),
            pltpu.VMEM((BLOCKS, 4, early, rows, lanes), BF16),
            pltpu.VMEM((BLOCKS, 9 * lanes, lanes), BF16),
            pltpu.VMEM((BLOCKS, TAPS * lanes, lanes), BF16),
            pltpu.VMEM((BLOCKS, 8, lanes), F32),
            pltpu.VMEM((BLOCKS, 4, 8, lanes), F32),
            pltpu.SemaphoreType.DMA((3,)),
            pltpu.SemaphoreType.DMA((PIECES,)),
            pltpu.SemaphoreType.DMA((BLOCKS, 4, PIECES)),
            pltpu.SemaphoreType.DMA((BLOCKS, 4, PIECES)),
            pltpu.SemaphoreType.DMA((BLOCKS, 4)),
            pltpu.SemaphoreType.DMA((BLOCKS, 4)),
            pltpu.SemaphoreType.DMA((BLOCKS, 4)),
            pltpu.SemaphoreType.DMA((BLOCKS, 4)),
        ],
        compiler_params=pltpu.CompilerParams(
            collective_id=0, has_side_effects=True, vmem_limit_bytes=48 << 20
        ),
        cost_estimate=pl.CostEstimate(flops=5_000_000_000, bytes_accessed=2_000_000, transcendentals=800_000),
    )(frames, clip_ids, norm_gain, space_kernel, time_kernel)


def solution(mesh):
    return jax.shard_map(
        per_device,
        mesh=mesh,
        in_specs=(P(("dp", "dev"), None, None), P(("dp", "dev")), P(), P(), P()),
        out_specs=P(("dp", "dev"), None, None),
        check_vma=False,
    )
```

time: 95.6 us -> 87.1 us (0.911)
  the two profiles are of different devices: /device:TPU:24 before, /device:TPU:6 now
where the time goes in v2:
time: 87.1 us; the launch traced here: 86.9 us
  Pallas kernels  85.4 us (98%)
  local copies, waits for them, and re-layouts  0.88 us (1%)
    pallas_call x1, Pallas kernels, per_device(): pl.pallas_call(kernel, out_shape=jax.ShapeDtypeStruct(frames.shape, BF16)...  85.4 us

profile of v2, /device:TPU:6, one launch (start us, length us, event | category | flops | bytes accessed | tf_op | source)
XLA Modules:
  0.0 86.9 jit_solution(4436714090247762269)
XLA Ops:
  0.7 85.4 %shard_map.55 = bf16[1,48,8192]{2,1,0:T(8,128)(2,1)S(1)} custom-call(bf16[1,48,8192]{2,1,0:T(8,128)(2,1)} %frames_hbm.1, s32[1]{0:T(128)S(6)} %copy.7.clip, f32[2,64]{1,0:T(2,128)} %gain_hbm.1, bf16[2,3,3,64,64]{4,3,2,1,0:T(8,128)(2,1)} %space_hbm.1, bf16[2,5,64,64]{3,2,1,0:T(8,128)(2,1)} %time_hbm.1), custom_call_target="tpu_custom_call" | custom-call | flops 5000000000 | bytes 2000000 | tf_op jit(solution)/shard_map/pallas_call | solution.py:328
  86.0 0.9 %copy.8 = bf16[1,48,8192]{2,1,0:T(8,128)(2,1)} copy(bf16[1,48,8192]{2,1,0:T(8,128)(2,1)S(1)} %shard_map.55) | data formatting | bytes 1572864

commit v3 on v2

--- a/solution.py
+++ b/solution.py
@@ -10,8 +10,9 @@
 STEP = 2
 GROUP = 2
 PIECES = 16
-EARLY = 3
-RAW_AT = 6
+EARLY = 4
+RAW_AT = 8
+RUNS = (((4, 8), (8, 12), (12, 16)), ((4, 8), (8, 12), (12, 15), (15, 16)))
 EPS = 1e-06
 MESH = pl.DeviceIdType.MESH
 F32 = jnp.float32
@@ -76,11 +77,19 @@
     for load in loads:
         load.start()
 
-    def copy(b, slot, p):
+    shifted[...] = jnp.zeros_like(shifted)
+    for r in range(3):
+        act[r, 0] = jnp.zeros((rows, lanes), BF16)
+        act[r, tiles + 1] = jnp.zeros((rows, lanes), BF16)
+    bands[...] = jnp.zeros_like(bands)
+
+    def copy(b, slot, run):
+        first, last = RUNS[b][run]
+        part = pl.ds(first * span, (last - first) * span)
         source = spat.at[b] if slot < 2 else came.at[b, slot - 2]
         return pltpu.make_async_remote_copy(
-            src_ref=source.at[piece(p)], dst_ref=came.at[b, slot, piece(p)],
-            send_sem=send_sem.at[b, slot, p], recv_sem=recv_sem.at[b, slot, p],
+            src_ref=source.at[part], dst_ref=came.at[b, slot, part],
+            send_sem=send_sem.at[b, slot, run], recv_sem=recv_sem.at[b, slot, run],
             device_id=peer(OFFSETS[slot % 2]), device_id_type=MESH,
         )
 
@@ -102,9 +111,15 @@
     lane = lax.broadcasted_iota(jnp.int32, (1, lanes), 1)
 
     def whole_group(sums):
+        sums = jnp.sum(sums, axis=0, keepdims=True)
         both = sums + pltpu.roll(sums, half, 1)
         beside = jnp.where(lane % 2 == 0, pltpu.roll(both, lanes - 1, 1), pltpu.roll(both, 1, 1))
         return both + beside
+
+    def by_eight(values):
+        return jnp.sum(values.reshape(-1, 8, lanes), axis=0)
+
+    no_sums = jnp.zeros((8, lanes), F32)
 
     def take(p, sums):
         fetch(p).wait()
@@ -112,20 +127,14 @@
             at = pl.multiple_of((p * span + t) * lanes, lanes)
             tile = frames[:, pl.ds(at, lanes)]
             x_buf[p * span + t] = tile
-            sums = sums + jnp.sum(tile.astype(F32), axis=0, keepdims=True)
+            sums = sums + by_eight(tile.astype(F32))
         return sums
 
-    sums = lax.fori_loop(0, EARLY + 1, take, jnp.zeros((1, lanes), F32))
+    sums = lax.fori_loop(0, EARLY + 1, take, no_sums)
     pl.semaphore_wait(barrier, sum(here(offset).astype(jnp.int32) for offset in OFFSETS))
     for slot in range(2):
         if_so(gives[slot], raw_copy(0, slot).start)
     sums = lax.fori_loop(EARLY + 1, PIECES, take, sums)
-
-    shifted[...] = jnp.zeros_like(shifted)
-    for r in range(3):
-        act[r, 0] = jnp.zeros((rows, lanes), BF16)
-        act[r, tiles + 1] = jnp.zeros((rows, lanes), BF16)
-    bands[...] = jnp.zeros_like(bands)
 
     def fill_bands(b):
         for r in range(3):
@@ -163,9 +172,9 @@
 
         def squares(p, total):
             off = x_buf[piece(p)].astype(F32) - mean
-            return total + jnp.sum(off * off, axis=(0, 1))[None]
-
-        spread = whole_group(lax.fori_loop(0, PIECES, squares, jnp.zeros((1, lanes), F32))) / table_entries
+            return total + by_eight(off * off)
+
+        spread = whole_group(lax.fori_loop(0, PIECES, squares, no_sums)) / table_entries
         gains = gain[b : b + 1]
         scale = lax.rsqrt(spread + EPS) * jnp.concatenate([gains, gains], 1) * 0.5
         facts[b, 0:1] = mean
@@ -186,8 +195,9 @@
                 own(p + 1)
 
             spat[b, piece(p)] = convolve(b, p)
-            for slot in range(2):
-                if_so(gives[slot], copy(b, slot, p).start)
+            for run, (_, last) in enumerate(RUNS[b]):
+                for slot in range(2):
+                    if_so(jnp.logical_and(p == last - 1, gives[slot]), copy(b, slot, run).start)
             return carry
 
         lax.fori_loop(EARLY, PIECES, make, 0)
@@ -238,13 +248,10 @@
         redo_or_blank(0)
         redo_or_blank(1)
 
-        def forward(p, carry):
+        for run in range(len(RUNS[b])):
             for slot in range(2):
-                if_so(takes[slot], copy(b, slot, p).wait_recv)
-                if_so(gives[slot + 2], copy(b, slot + 2, p).start)
-            return carry
-
-        lax.fori_loop(EARLY, PIECES, forward, 0)
+                if_so(takes[slot], copy(b, slot, run).wait_recv)
+                if_so(gives[slot + 2], copy(b, slot + 2, run).start)
 
         redo_or_blank(2)
         redo_or_blank(3)
@@ -281,7 +288,7 @@
             value = (x_buf[piece(p)].astype(F32) + update.reshape(span, rows, lanes)).astype(BF16)
             if b + 1 < BLOCKS:
                 x_buf[piece(p)] = value
-                return sums + jnp.sum(value.astype(F32), axis=(0, 1))[None]
+                return sums + by_eight(value.astype(F32))
             for t in range(span):
                 at = pl.multiple_of((p * span + t) * lanes, lanes)
                 out[0, :, pl.ds(at, lanes)] = value[t]
@@ -293,11 +300,12 @@
                 for slot in range(2):
                     if_so(jnp.logical_and(p == RAW_AT, gives[slot]), raw_copy(b + 1, slot).start)
 
-            for slot in (2, 3):
-                if_so(takes[slot], copy(b, slot, p).wait_recv)
+            for run, (first, _) in enumerate(RUNS[b]):
+                for slot in (2, 3):
+                    if_so(jnp.logical_and(p == first, takes[slot]), copy(b, slot, run).wait_recv)
             return finish(p, sums)
 
-        sums = lax.fori_loop(0, EARLY, finish, jnp.zeros((1, lanes), F32))
+        sums = lax.fori_loop(0, EARLY, finish, no_sums)
         sums = lax.fori_loop(EARLY, PIECES, finish_arrived, sums)
 
     for b in range(BLOCKS):
@@ -306,13 +314,8 @@
             if b > 0 or slot > 1:
                 if_so(gives[slot], raw_copy(b, slot).wait_send)
 
-    def drain(p, carry):
-        for b in range(BLOCKS):
-            for slot in range(4):
-                if_so(gives[slot], copy(b, slot, p).wait_send)
-        return carry
-
-    lax.fori_loop(EARLY, PIECES, drain, 0)
+            for run in range(len(RUNS[b])):
+                if_so(gives[slot], copy(b, slot, run).wait_send)
 
 
 def per_device(frames, clip_ids, norm_gain, space_kernel, time_kernel):
@@ -347,8 +350,8 @@
             pltpu.VMEM((BLOCKS, 4, 8, lanes), F32),
             pltpu.SemaphoreType.DMA((3,)),
             pltpu.SemaphoreType.DMA((PIECES,)),
-            pltpu.SemaphoreType.DMA((BLOCKS, 4, PIECES)),
-            pltpu.SemaphoreType.DMA((BLOCKS, 4, PIECES)),
+            pltpu.SemaphoreType.DMA((BLOCKS, 4, 4)),
+            pltpu.SemaphoreType.DMA((BLOCKS, 4, 4)),
             pltpu.SemaphoreType.DMA((BLOCKS, 4)),
             pltpu.SemaphoreType.DMA((BLOCKS, 4)),
             pltpu.SemaphoreType.DMA((BLOCKS, 4)),

time: 87.1 us -> 86.1 us (0.989)
  Pallas kernels: 85.4 us -> 84.4 us
    pallas_call x1, Pallas kernels: 85.4 us -> 84.4 us  [per_device(): pl.pallas_call(kernel, out_shape=jax.ShapeDtypeStruct(frames.shape, BF16)...]
where the time goes in v3:
time: 86.1 us; the launch traced here: 85.9 us
  Pallas kernels  84.4 us (98%)
  local copies, waits for them, and re-layouts  0.88 us (1%)
    pallas_call x1, Pallas kernels, per_device(): pl.pallas_call(kernel, out_shape=jax.ShapeDtypeStruct(frames.shape, BF16)...  84.4 us

profile of v3, /device:TPU:6, one launch (start us, length us, event | category | flops | bytes accessed | tf_op | source)
XLA Modules:
  0.0 85.9 jit_solution(168935024012389438)
XLA Ops:
  0.7 84.4 %shard_map.55 = bf16[1,48,8192]{2,1,0:T(8,128)(2,1)S(1)} custom-call(bf16[1,48,8192]{2,1,0:T(8,128)(2,1)} %frames_hbm.1, s32[1]{0:T(128)S(6)} %copy.7.clip, f32[2,64]{1,0:T(2,128)} %gain_hbm.1, bf16[2,3,3,64,64]{4,3,2,1,0:T(8,128)(2,1)} %space_hbm.1, bf16[2,5,64,64]{3,2,1,0:T(8,128)(2,1)} %time_hbm.1), custom_call_target="tpu_custom_call" | custom-call | flops 5000000000 | bytes 2000000 | tf_op jit(solution)/shard_map/pallas_call | solution.py:331
  85.0 0.9 %copy.8 = bf16[1,48,8192]{2,1,0:T(8,128)(2,1)} copy(bf16[1,48,8192]{2,1,0:T(8,128)(2,1)S(1)} %shard_map.55) | data formatting | bytes 1572864

commit v4 on v3

--- a/solution.py
+++ b/solution.py
@@ -12,6 +12,7 @@
 PIECES = 16
 EARLY = 4
 RAW_AT = 8
+LINE = 32
 RUNS = (((4, 8), (8, 12), (12, 16)), ((4, 8), (8, 12), (12, 15), (15, 16)))
 EPS = 1e-06
 MESH = pl.DeviceIdType.MESH
@@ -24,8 +25,9 @@
 def kernel(
     frames_hbm, clip, gain_hbm, space_hbm, time_hbm, out,
     frames, gain, space, time,
-    x_buf, shifted, act, spat, came, raw, bands, taps, facts, facts_in,
+    x_buf, shifted, act, spat, came, raw, bands, taps, facts, facts_in, passing,
     load_sem, frame_sem, send_sem, recv_sem, raw_send, raw_recv, fact_send, fact_recv,
+    pass_send, pass_recv, ready,
 ):
     count = lax.axis_size("dev")
     me = lax.axis_index("dev")
@@ -49,12 +51,24 @@
     def if_so(condition, action):
         pl.when(condition)(action)
 
+    line = me // LINE
+    at_start = lax.rem(me, LINE) < STEP
+    at_end = lax.rem(me, LINE) >= LINE - STEP
+    sends_aside = jnp.logical_and(at_end, me + LINE < count)
+    passes_on = jnp.logical_and(at_end, me >= LINE)
+    from_aside = jnp.logical_and(at_start, me >= LINE)
+
+    def aside(run, source_line):
+        return run >= 2 - source_line
+
     barrier = pltpu.get_barrier_semaphore()
-    for offset in OFFSETS:
-
-        @pl.when(here(offset))
-        def _():
-            pl.semaphore_signal(barrier, inc=1, device_id=peer(offset), device_id_type=MESH)
+
+    def arrive(offset):
+        pl.semaphore_signal(barrier, inc=1, device_id=peer(offset), device_id_type=MESH)
+
+    if_so(here(-STEP), lambda: arrive(-STEP))
+    if_so(passes_on, lambda: arrive(-LINE))
+    if_so(from_aside, lambda: arrive(LINE - STEP))
 
     def piece(p):
         return pl.ds(pl.multiple_of(p * span, span), span)
@@ -102,10 +116,29 @@
         )
 
     def fact_copy(b, slot):
+        source = facts.at[b] if slot < 2 else facts_in.at[b, slot - 2]
         return pltpu.make_async_remote_copy(
-            src_ref=facts.at[b], dst_ref=facts_in.at[b, slot],
+            src_ref=source, dst_ref=facts_in.at[b, slot],
             send_sem=fact_send.at[b, slot], recv_sem=fact_recv.at[b, slot],
-            device_id=peer(OFFSETS[slot]), device_id_type=MESH,
+            device_id=peer(OFFSETS[slot % 2]), device_id_type=MESH,
+        )
+
+    def copy_aside(b, run):
+        first, last = RUNS[b][run]
+        part = pl.ds(first * span, (last - first) * span)
+        return pltpu.make_async_remote_copy(
+            src_ref=spat.at[b, part], dst_ref=passing.at[b, part],
+            send_sem=send_sem.at[b, 0, run], recv_sem=pass_recv.at[b, run],
+            device_id=peer(LINE), device_id_type=MESH,
+        )
+
+    def pass_on(b, run):
+        first, last = RUNS[b][run]
+        part = pl.ds(first * span, (last - first) * span)
+        return pltpu.make_async_remote_copy(
+            src_ref=passing.at[b, part], dst_ref=came.at[b, 0, part],
+            send_sem=pass_send.at[b, run], recv_sem=recv_sem.at[b, 0, run],
+            device_id=peer(STEP - LINE), device_id_type=MESH,
         )
 
     lane = lax.broadcasted_iota(jnp.int32, (1, lanes), 1)
@@ -131,9 +164,20 @@
         return sums
 
     sums = lax.fori_loop(0, EARLY + 1, take, no_sums)
-    pl.semaphore_wait(barrier, sum(here(offset).astype(jnp.int32) for offset in OFFSETS))
-    for slot in range(2):
-        if_so(gives[slot], raw_copy(0, slot).start)
+    pl.semaphore_wait(barrier, sum(c.astype(jnp.int32) for c in (gives[0], sends_aside, passes_on)))
+
+    @pl.when(gives[0])
+    def _():
+        pl.semaphore_signal(ready, inc=1, device_id=peer(STEP), device_id_type=MESH)
+        raw_copy(0, 0).start()
+
+    soon = jnp.logical_and(gives[1], jnp.logical_not(at_start))
+    late = jnp.logical_and(gives[1], at_start)
+
+    @pl.when(soon)
+    def _():
+        pl.semaphore_wait(ready, 1)
+        raw_copy(0, 1).start()
     sums = lax.fori_loop(EARLY + 1, PIECES, take, sums)
 
     def fill_bands(b):
@@ -180,8 +224,9 @@
         facts[b, 0:1] = mean
         facts[b, 1:2] = scale
         facts[b, 2:8] = jnp.full((6, lanes), clip[0], jnp.int32).astype(F32)
-        for slot in range(4):
-            if_so(here(OFFSETS[slot]), fact_copy(b, slot).start)
+        down = soon if b == 0 else gives[1]
+        if_so(gives[0], fact_copy(b, 0).start)
+        if_so(down, fact_copy(b, 1).start)
 
         def own(p):
             activate(x_buf[piece(p)], p * span, mean, scale)
@@ -196,15 +241,32 @@
 
             spat[b, piece(p)] = convolve(b, p)
             for run, (_, last) in enumerate(RUNS[b]):
-                for slot in range(2):
-                    if_so(jnp.logical_and(p == last - 1, gives[slot]), copy(b, slot, run).start)
+
+                @pl.when(p == last - 1)
+                def _():
+                    away = jnp.logical_and(sends_aside, aside(run, line))
+                    if_so(away, copy_aside(b, run).start)
+                    if_so(jnp.logical_and(gives[0], jnp.logical_not(away)), copy(b, 0, run).start)
+                    if_so(down, copy(b, 1, run).start)
+
             return carry
 
         lax.fori_loop(EARLY, PIECES, make, 0)
 
+        if b == 0:
+
+            @pl.when(late)
+            def _():
+                pl.semaphore_wait(ready, 1)
+                raw_copy(b, 1).start()
+                fact_copy(b, 1).start()
+                for run in range(len(RUNS[b])):
+                    copy(b, 1, run).start()
+
         for slot in range(2):
-            if_so(takes[slot], raw_copy(b, slot).wait_recv)
-            if_so(gives[slot + 2], raw_copy(b, slot + 2).start)
+            for what in (raw_copy, fact_copy):
+                if_so(takes[slot], what(b, slot).wait_recv)
+                if_so(gives[slot + 2], what(b, slot + 2).start)
 
         def own_early(p, carry):
             own(p)
@@ -221,7 +283,7 @@
         def redo(slot):
             if slot > 1:
                 raw_copy(b, slot).wait_recv()
-            fact_copy(b, slot).wait_recv()
+                fact_copy(b, slot).wait_recv()
             mean = facts_in[b, slot, 0:1]
             scale = facts_in[b, slot, 1:2]
 
@@ -252,6 +314,12 @@
             for slot in range(2):
                 if_so(takes[slot], copy(b, slot, run).wait_recv)
                 if_so(gives[slot + 2], copy(b, slot + 2, run).start)
+
+            @pl.when(jnp.logical_and(passes_on, aside(run, line - 1)))
+            def _():
+                copy_aside(b, run).wait_recv()
+                pass_on(b, run).start()
+
 
         redo_or_blank(2)
         redo_or_blank(3)
@@ -310,12 +378,14 @@
 
     for b in range(BLOCKS):
         for slot in range(4):
-            if_so(here(OFFSETS[slot]), fact_copy(b, slot).wait_send)
+            if_so(gives[slot], fact_copy(b, slot).wait_send)
             if b > 0 or slot > 1:
                 if_so(gives[slot], raw_copy(b, slot).wait_send)
 
             for run in range(len(RUNS[b])):
                 if_so(gives[slot], copy(b, slot, run).wait_send)
+        for run in range(len(RUNS[b])):
+            if_so(jnp.logical_and(passes_on, aside(run, line - 1)), pass_on(b, run).wait_send)
 
 
 def per_device(frames, clip_ids, norm_gain, space_kernel, time_kernel):
@@ -348,6 +418,7 @@
             pltpu.VMEM((BLOCKS, TAPS * lanes, lanes), BF16),
             pltpu.VMEM((BLOCKS, 8, lanes), F32),
             pltpu.VMEM((BLOCKS, 4, 8, lanes), F32),
+            pltpu.VMEM((BLOCKS, tiles, rows, lanes), BF16),
             pltpu.SemaphoreType.DMA((3,)),
             pltpu.SemaphoreType.DMA((PIECES,)),
             pltpu.SemaphoreType.DMA((BLOCKS, 4, 4)),
@@ -356,6 +427,9 @@
             pltpu.SemaphoreType.DMA((BLOCKS, 4)),
             pltpu.SemaphoreType.DMA((BLOCKS, 4)),
             pltpu.SemaphoreType.DMA((BLOCKS, 4)),
+            pltpu.SemaphoreType.DMA((BLOCKS, 4)),
+            pltpu.SemaphoreType.DMA((BLOCKS, 4)),
+            pltpu.SemaphoreType.REGULAR,
         ],
         compiler_params=pltpu.CompilerParams(
             collective_id=0, has_side_effects=True, vmem_limit_bytes=48 << 20

time: 86.1 us -> 92.1 us (1.070)
  the two profiles are of different devices: /device:TPU:6 before, /device:TPU:20 now
where the time goes in v4:
time: 92.1 us; the launch traced here: 91.9 us
  Pallas kernels  90.4 us (98%)
    pallas_call x1, Pallas kernels, per_device(): pl.pallas_call(kernel, out_shape=jax.ShapeDtypeStruct(frames.shape, BF16)...  90.4 us

profile of v4, /device:TPU:20, one launch (start us, length us, event | category | flops | bytes accessed | tf_op | source)
XLA Modules:
  0.0 91.9 jit_solution(11833215641356943128)
XLA Ops:
  0.7 90.4 %shard_map.55 = bf16[1,48,8192]{2,1,0:T(8,128)(2,1)S(1)} custom-call(bf16[1,48,8192]{2,1,0:T(8,128)(2,1)} %frames_hbm.1, s32[1]{0:T(128)S(6)} %copy.7.clip, f32[2,64]{1,0:T(2,128)} %gain_hbm.1, bf16[2,3,3,64,64]{4,3,2,1,0:T(8,128)(2,1)} %space_hbm.1, bf16[2,5,64,64]{3,2,1,0:T(8,128)(2,1)} %time_hbm.1), custom_call_target="tpu_custom_call" | custom-call | flops 5000000000 | bytes 2000000 | tf_op jit(solution)/shard_map/pallas_call | solution.py:401
  91.0 0.9 copy.8

commit v5 on v4

--- a/solution.py
+++ b/solution.py
@@ -55,11 +55,15 @@
     at_start = lax.rem(me, LINE) < STEP
     at_end = lax.rem(me, LINE) >= LINE - STEP
     sends_aside = jnp.logical_and(at_end, me + LINE < count)
-    passes_on = jnp.logical_and(at_end, me >= LINE)
+    passes_on = me >= count - STEP
     from_aside = jnp.logical_and(at_start, me >= LINE)
 
-    def aside(run, source_line):
-        return run >= 2 - source_line
+    core = lax.rem(me, STEP)
+
+    def aside(run):
+        return run >= 2
+
+    seams = range(count // LINE - 1)
 
     barrier = pltpu.get_barrier_semaphore()
 
@@ -67,8 +71,9 @@
         pl.semaphore_signal(barrier, inc=1, device_id=peer(offset), device_id_type=MESH)
 
     if_so(here(-STEP), lambda: arrive(-STEP))
-    if_so(passes_on, lambda: arrive(-LINE))
-    if_so(from_aside, lambda: arrive(LINE - STEP))
+    for seam in seams:
+        if_so(passes_on, lambda: arrive((seam + 1) * LINE - count))
+    if_so(from_aside, lambda: arrive(count - STEP + core - me))
 
     def piece(p):
         return pl.ds(pl.multiple_of(p * span, span), span)
@@ -123,22 +128,22 @@
             device_id=peer(OFFSETS[slot % 2]), device_id_type=MESH,
         )
 
-    def copy_aside(b, run):
+    def copy_aside(b, seam, run):
         first, last = RUNS[b][run]
         part = pl.ds(first * span, (last - first) * span)
         return pltpu.make_async_remote_copy(
-            src_ref=spat.at[b, part], dst_ref=passing.at[b, part],
-            send_sem=send_sem.at[b, 0, run], recv_sem=pass_recv.at[b, run],
-            device_id=peer(LINE), device_id_type=MESH,
-        )
-
-    def pass_on(b, run):
+            src_ref=spat.at[b, part], dst_ref=passing.at[b, seam, part],
+            send_sem=send_sem.at[b, 0, run], recv_sem=pass_recv.at[b, seam, run],
+            device_id={"dev": count - STEP + core}, device_id_type=MESH,
+        )
+
+    def pass_on(b, seam, run):
         first, last = RUNS[b][run]
         part = pl.ds(first * span, (last - first) * span)
         return pltpu.make_async_remote_copy(
-            src_ref=passing.at[b, part], dst_ref=came.at[b, 0, part],
-            send_sem=pass_send.at[b, run], recv_sem=recv_sem.at[b, 0, run],
-            device_id=peer(STEP - LINE), device_id_type=MESH,
+            src_ref=passing.at[b, seam, part], dst_ref=came.at[b, 0, part],
+            send_sem=pass_send.at[b, seam, run], recv_sem=recv_sem.at[b, 0, run],
+            device_id={"dev": (seam + 1) * LINE + core}, device_id_type=MESH,
         )
 
     lane = lax.broadcasted_iota(jnp.int32, (1, lanes), 1)
@@ -164,7 +169,7 @@
         return sums
 
     sums = lax.fori_loop(0, EARLY + 1, take, no_sums)
-    pl.semaphore_wait(barrier, sum(c.astype(jnp.int32) for c in (gives[0], sends_aside, passes_on)))
+    pl.semaphore_wait(barrier, sum(n * c.astype(jnp.int32) for n, c in ((1, gives[0]), (1, sends_aside), (len(seams), passes_on))))
 
     @pl.when(gives[0])
     def _():
@@ -244,9 +249,11 @@
 
                 @pl.when(p == last - 1)
                 def _():
-                    away = jnp.logical_and(sends_aside, aside(run, line))
-                    if_so(away, copy_aside(b, run).start)
-                    if_so(jnp.logical_and(gives[0], jnp.logical_not(away)), copy(b, 0, run).start)
+                    if aside(run):
+                        if_so(sends_aside, copy_aside(b, lax.rem(line, len(seams)), run).start)
+                        if_so(jnp.logical_and(gives[0], jnp.logical_not(sends_aside)), copy(b, 0, run).start)
+                    else:
+                        if_so(gives[0], copy(b, 0, run).start)
                     if_so(down, copy(b, 1, run).start)
 
             return carry
@@ -310,15 +317,17 @@
         redo_or_blank(0)
         redo_or_blank(1)
 
+        @pl.when(passes_on)
+        def _():
+            for run in filter(aside, range(len(RUNS[b]))):
+                for seam in seams:
+                    copy_aside(b, seam, run).wait_recv()
+                    pass_on(b, seam, run).start()
+
         for run in range(len(RUNS[b])):
             for slot in range(2):
                 if_so(takes[slot], copy(b, slot, run).wait_recv)
                 if_so(gives[slot + 2], copy(b, slot + 2, run).start)
-
-            @pl.when(jnp.logical_and(passes_on, aside(run, line - 1)))
-            def _():
-                copy_aside(b, run).wait_recv()
-                pass_on(b, run).start()
 
 
         redo_or_blank(2)
@@ -384,8 +393,9 @@
 
             for run in range(len(RUNS[b])):
                 if_so(gives[slot], copy(b, slot, run).wait_send)
-        for run in range(len(RUNS[b])):
-            if_so(jnp.logical_and(passes_on, aside(run, line - 1)), pass_on(b, run).wait_send)
+        for run in filter(aside, range(len(RUNS[b]))):
+            for seam in seams:
+                if_so(passes_on, pass_on(b, seam, run).wait_send)
 
 
 def per_device(frames, clip_ids, norm_gain, space_kernel, time_kernel):
@@ -418,7 +428,7 @@
             pltpu.VMEM((BLOCKS, TAPS * lanes, lanes), BF16),
             pltpu.VMEM((BLOCKS, 8, lanes), F32),
             pltpu.VMEM((BLOCKS, 4, 8, lanes), F32),
-            pltpu.VMEM((BLOCKS, tiles, rows, lanes), BF16),
+            pltpu.VMEM((BLOCKS, 3, tiles, rows, lanes), BF16),
             pltpu.SemaphoreType.DMA((3,)),
             pltpu.SemaphoreType.DMA((PIECES,)),
             pltpu.SemaphoreType.DMA((BLOCKS, 4, 4)),
@@ -427,8 +437,8 @@
             pltpu.SemaphoreType.DMA((BLOCKS, 4)),
             pltpu.SemaphoreType.DMA((BLOCKS, 4)),
             pltpu.SemaphoreType.DMA((BLOCKS, 4)),
-            pltpu.SemaphoreType.DMA((BLOCKS, 4)),
-            pltpu.SemaphoreType.DMA((BLOCKS, 4)),
+            pltpu.SemaphoreType.DMA((BLOCKS, 3, 4)),
+            pltpu.SemaphoreType.DMA((BLOCKS, 3, 4)),
             pltpu.SemaphoreType.REGULAR,
         ],
         compiler_params=pltpu.CompilerParams(

time: 92.1 us -> 139 us (1.51)
  the two profiles are of different devices: /device:TPU:20 before, /device:TPU:6 now
where the time goes in v5:
time: 139 us; the launch traced here: 138 us
  Pallas kernels  137 us (99%)
    pallas_call x1, Pallas kernels, per_device(): pl.pallas_call(kernel, out_shape=jax.ShapeDtypeStruct(frames.shape, BF16)...  137 us

profile of v5, /device:TPU:6, one launch (start us, length us, event | category | flops | bytes accessed | tf_op | source)
XLA Modules:
  0.0 138.2 jit_solution(52771581446157550)
XLA Ops:
  0.7 136.7 %shard_map.55 = bf16[1,48,8192]{2,1,0:T(8,128)(2,1)S(1)} custom-call(bf16[1,48,8192]{2,1,0:T(8,128)(2,1)} %frames_hbm.1, s32[1]{0:T(128)S(6)} %copy.7.clip, f32[2,64]{1,0:T(2,128)} %gain_hbm.1, bf16[2,3,3,64,64]{4,3,2,1,0:T(8,128)(2,1)} %space_hbm.1, bf16[2,5,64,64]{3,2,1,0:T(8,128)(2,1)} %time_hbm.1), custom_call_target="tpu_custom_call" | custom-call | flops 5000000000 | bytes 2000000 | tf_op jit(solution)/shard_map/pallas_call | solution.py:411
  137.4 0.9 copy.8

commit v6 on v3

--- a/solution.py
+++ b/solution.py
@@ -12,7 +12,7 @@
 PIECES = 16
 EARLY = 4
 RAW_AT = 8
-RUNS = (((4, 8), (8, 12), (12, 16)), ((4, 8), (8, 12), (12, 15), (15, 16)))
+RUNS = (((0, 4), (4, 8), (8, 12), (12, 16)), ((0, 4), (4, 8), (8, 12), (12, 15), (15, 16)))
 EPS = 1e-06
 MESH = pl.DeviceIdType.MESH
 F32 = jnp.float32
@@ -94,9 +94,8 @@
         )
 
     def raw_copy(b, slot):
-        source = x_buf.at[pl.ds(0, early)] if slot < 2 else raw.at[b, slot - 2]
         return pltpu.make_async_remote_copy(
-            src_ref=source, dst_ref=raw.at[b, slot],
+            src_ref=x_buf.at[pl.ds(0, early)], dst_ref=raw.at[b, slot],
             send_sem=raw_send.at[b, slot], recv_sem=raw_recv.at[b, slot],
             device_id=peer(OFFSETS[slot % 2]), device_id_type=MESH,
         )
@@ -180,7 +179,7 @@
         facts[b, 0:1] = mean
         facts[b, 1:2] = scale
         facts[b, 2:8] = jnp.full((6, lanes), clip[0], jnp.int32).astype(F32)
-        for slot in range(4):
+        for slot in range(4 if b == 0 else 2):
             if_so(here(OFFSETS[slot]), fact_copy(b, slot).start)
 
         def own(p):
@@ -196,7 +195,7 @@
 
             spat[b, piece(p)] = convolve(b, p)
             for run, (_, last) in enumerate(RUNS[b]):
-                for slot in range(2):
+                for slot in range(2 if run else 0):
                     if_so(jnp.logical_and(p == last - 1, gives[slot]), copy(b, slot, run).start)
             return carry
 
@@ -204,7 +203,6 @@
 
         for slot in range(2):
             if_so(takes[slot], raw_copy(b, slot).wait_recv)
-            if_so(gives[slot + 2], raw_copy(b, slot + 2).start)
 
         def own_early(p, carry):
             own(p)
@@ -220,7 +218,10 @@
 
         def redo(slot):
             if slot > 1:
-                raw_copy(b, slot).wait_recv()
+                if b == 0:
+                    fact_copy(b, slot).wait_recv()
+                copy(b, slot, 0).wait_recv()
+                return
             fact_copy(b, slot).wait_recv()
             mean = facts_in[b, slot, 0:1]
             scale = facts_in[b, slot, 1:2]
@@ -250,7 +251,8 @@
 
         for run in range(len(RUNS[b])):
             for slot in range(2):
-                if_so(takes[slot], copy(b, slot, run).wait_recv)
+                if run:
+                    if_so(takes[slot], copy(b, slot, run).wait_recv)
                 if_so(gives[slot + 2], copy(b, slot + 2, run).start)
 
         redo_or_blank(2)
@@ -300,7 +302,7 @@
                 for slot in range(2):
                     if_so(jnp.logical_and(p == RAW_AT, gives[slot]), raw_copy(b + 1, slot).start)
 
-            for run, (first, _) in enumerate(RUNS[b]):
+            for run, (first, _) in list(enumerate(RUNS[b]))[1:]:
                 for slot in (2, 3):
                     if_so(jnp.logical_and(p == first, takes[slot]), copy(b, slot, run).wait_recv)
             return finish(p, sums)
@@ -310,11 +312,11 @@
 
     for b in range(BLOCKS):
         for slot in range(4):
-            if_so(here(OFFSETS[slot]), fact_copy(b, slot).wait_send)
-            if b > 0 or slot > 1:
+            if b == 0 or slot < 2:
+                if_so(here(OFFSETS[slot]), fact_copy(b, slot).wait_send)
+            if b > 0 and slot < 2:
                 if_so(gives[slot], raw_copy(b, slot).wait_send)
-
-            for run in range(len(RUNS[b])):
+            for run in range(1 if slot < 2 else 0, len(RUNS[b])):
                 if_so(gives[slot], copy(b, slot, run).wait_send)
 
 
@@ -343,15 +345,15 @@
             pltpu.VMEM((3, tiles + 2, rows, lanes), BF16),
             pltpu.VMEM((BLOCKS, tiles, rows, lanes), BF16),
             pltpu.VMEM((BLOCKS, 4, tiles, rows, lanes), BF16),
-            pltpu.VMEM((BLOCKS, 4, early, rows, lanes), BF16),
+            pltpu.VMEM((BLOCKS, 2, early, rows, lanes), BF16),
             pltpu.VMEM((BLOCKS, 9 * lanes, lanes), BF16),
             pltpu.VMEM((BLOCKS, TAPS * lanes, lanes), BF16),
             pltpu.VMEM((BLOCKS, 8, lanes), F32),
             pltpu.VMEM((BLOCKS, 4, 8, lanes), F32),
             pltpu.SemaphoreType.DMA((3,)),
             pltpu.SemaphoreType.DMA((PIECES,)),
-            pltpu.SemaphoreType.DMA((BLOCKS, 4, 4)),
-            pltpu.SemaphoreType.DMA((BLOCKS, 4, 4)),
+            pltpu.SemaphoreType.DMA((BLOCKS, 4, 5)),
+            pltpu.SemaphoreType.DMA((BLOCKS, 4, 5)),
             pltpu.SemaphoreType.DMA((BLOCKS, 4)),
             pltpu.SemaphoreType.DMA((BLOCKS, 4)),
             pltpu.SemaphoreType.DMA((BLOCKS, 4)),

time: 86.1 us -> 85.6 us (level)
  no operation moved by 1% of the time
where the time goes in v6:
time: 85.6 us; the launch traced here: 85.4 us
  Pallas kernels  83.9 us (98%)
  local copies, waits for them, and re-layouts  0.88 us (1%)
    pallas_call x1, Pallas kernels, per_device(): pl.pallas_call(kernel, out_shape=jax.ShapeDtypeStruct(frames.shape, BF16)...  83.9 us

profile of v6, /device:TPU:6, one launch (start us, length us, event | category | flops | bytes accessed | tf_op | source)
XLA Modules:
  0.0 85.4 jit_solution(9864562656247266043)
XLA Ops:
  0.7 83.9 %shard_map.55 = bf16[1,48,8192]{2,1,0:T(8,128)(2,1)S(1)} custom-call(bf16[1,48,8192]{2,1,0:T(8,128)(2,1)} %frames_hbm.1, s32[1]{0:T(128)S(6)} %copy.7.clip, f32[2,64]{1,0:T(2,128)} %gain_hbm.1, bf16[2,3,3,64,64]{4,3,2,1,0:T(8,128)(2,1)} %space_hbm.1, bf16[2,5,64,64]{3,2,1,0:T(8,128)(2,1)} %time_hbm.1), custom_call_target="tpu_custom_call" | custom-call | flops 5000000000 | bytes 2000000 | tf_op jit(solution)/shard_map/pallas_call | solution.py:333
  84.6 0.9 %copy.8 = bf16[1,48,8192]{2,1,0:T(8,128)(2,1)} copy(bf16[1,48,8192]{2,1,0:T(8,128)(2,1)S(1)} %shard_map.55) | data formatting | bytes 1572864

commit v7 on v6

--- a/solution.py
+++ b/solution.py
@@ -12,7 +12,7 @@
 PIECES = 16
 EARLY = 4
 RAW_AT = 8
-RUNS = (((0, 4), (4, 8), (8, 12), (12, 16)), ((0, 4), (4, 8), (8, 12), (12, 15), (15, 16)))
+RUNS = (((0, 4), (4, 9), (9, 16)), ((0, 4), (4, 8), (8, 12), (12, 15), (15, 16)))
 EPS = 1e-06
 MESH = pl.DeviceIdType.MESH
 F32 = jnp.float32

time: 85.6 us -> 86.3 us (level)
  no operation moved by 1% of the time
where the time goes in v7:
time: 86.3 us; the launch traced here: 86.2 us
  Pallas kernels  84.7 us (98%)
  local copies, waits for them, and re-layouts  0.88 us (1%)
    pallas_call x1, Pallas kernels, per_device(): pl.pallas_call(kernel, out_shape=jax.ShapeDtypeStruct(frames.shape, BF16)...  84.7 us

profile of v7, /device:TPU:6, one launch (start us, length us, event | category | flops | bytes accessed | tf_op | source)
XLA Modules:
  0.0 86.2 jit_solution(6259249269177490913)
XLA Ops:
  0.7 84.7 %shard_map.55 = bf16[1,48,8192]{2,1,0:T(8,128)(2,1)S(1)} custom-call(bf16[1,48,8192]{2,1,0:T(8,128)(2,1)} %frames_hbm.1, s32[1]{0:T(128)S(6)} %copy.7.clip, f32[2,64]{1,0:T(2,128)} %gain_hbm.1, bf16[2,3,3,64,64]{4,3,2,1,0:T(8,128)(2,1)} %space_hbm.1, bf16[2,5,64,64]{3,2,1,0:T(8,128)(2,1)} %time_hbm.1), custom_call_target="tpu_custom_call" | custom-call | flops 5000000000 | bytes 2000000 | tf_op jit(solution)/shard_map/pallas_call | solution.py:333
  85.3 0.9 %copy.8 = bf16[1,48,8192]{2,1,0:T(8,128)(2,1)} copy(bf16[1,48,8192]{2,1,0:T(8,128)(2,1)S(1)} %shard_map.55) | data formatting | bytes 1572864
